TPU v7x, 32 devices: a whole 2x2x4 slice. The times are simulated.
32 devices in a mesh: events: 4 (over z), nodes: 8 (over y, x, core).
Axes of the slice: x: 2, y: 2, z: 4, core: 2. Of those that a mesh axis runs over, the one named last changes fastest.
Arguments:
- nodes_in: bfloat16 [4, 16384, 128], P('events', 'nodes'), may hold values from -6 to 6
- edge_latents: bfloat16 [4, 8, 8, 2, 128, 128], P('events', 'nodes'), may hold values from -6 to 6
- src_block: int32 [4, 8, 8, 2], P('events', 'nodes'), may hold values from 0 to 15
- src_offset: int32 [4, 8, 8, 2, 128], P('events', 'nodes'), may hold values from 0 to 127
- dst_block: int32 [4, 8, 8, 2], P('events', 'nodes'), may hold values from 0 to 15
- dst_offset: int32 [4, 8, 8, 2, 128], P('events', 'nodes'), may hold values from 0 to 127
- tile_counts: int32 [4, 8, 8], P('events'), may hold values from 1 to 2, as said below
- w_edge1: bfloat16 [384, 128], replicated, may hold values from -0.3125 to 0.3125
- b_edge1: float32 [128], replicated, may hold values from -3 to 3
- w_edge2: bfloat16 [128, 128], replicated, may hold values from -0.5 to 0.5
- b_edge2: float32 [128], replicated, may hold values from -3 to 3
- w_node1: bfloat16 [256, 128], replicated, may hold values from -0.375 to 0.375
- b_node1: float32 [128], replicated, may hold values from -3 to 3
- w_node2: bfloat16 [128, 128], replicated, may hold values from -0.5 to 0.5
- b_node2: float32 [128], replicated, may hold values from -3 to 3
- cotangent: bfloat16 [4, 16384, 128], P('events', 'nodes'), may hold values from -6 to 6
Outputs:
- new_nodes: bfloat16 [4, 16384, 128], P('events', 'nodes')
- node_grads: bfloat16 [4, 16384, 128], P('events', 'nodes')
- grad_w_edge1: float32 [384, 128], replicated
- grad_b_edge1: float32 [128], replicated
- grad_w_edge2: float32 [128, 128], replicated
- grad_b_edge2: float32 [128], replicated
- grad_w_node1: float32 [256, 128], replicated
- grad_b_node1: float32 [128], replicated
- grad_w_node2: float32 [128, 128], replicated
- grad_b_node2: float32 [128], replicated
Inputs may be any that keep to these rules, and one draw needn't show every extreme that they name: tile_counts[g, s, d] is the number of live slots from source device s to destination device d; in every event group some destination device receives exactly 2 tiles from every source device.
All inputs are finite; a program needn't handle non-finite values.
Results may differ from a plain program's by a relative error of at most 0.0067.
Values may be sent and summed in bfloat16 or wider, within the bound.
A program may use at most 64 MiB of HBM per device.

v0:
```python
import jax
import jax.numpy as jnp
from jax import lax
from jax.sharding import PartitionSpec as P


def silu_slope(value):
    sig = jax.nn.sigmoid(value)
    return sig * (1.0 + value * (1.0 - sig))


def tile_onehot(offsets, tile):
    return (offsets[..., None] == jnp.arange(tile, dtype=jnp.int32)[None, None, :]).astype(
        jnp.bfloat16
    )


def gather_tiles(table, blocks, onehot):
    tile = onehot.shape[-1]
    picked = table.reshape(-1, tile, table.shape[-1])[blocks]
    return jnp.einsum("ten,tnd->ted", onehot, picked, preferred_element_type=jnp.float32).astype(
        table.dtype
    )


def scatter_tiles(values, blocks, onehot, block_count):
    if values.dtype == jnp.bfloat16:
        per_tile = jnp.einsum("ten,ted->tnd", onehot, values, preferred_element_type=jnp.float32)
    else:
        per_tile = jnp.einsum(
            "ten,ted->tnd", onehot.astype(jnp.float32), values, precision=lax.Precision.HIGHEST
        )
    picker = (blocks[:, None] == jnp.arange(block_count, dtype=jnp.int32)[None, :]).astype(
        jnp.float32
    )
    summed = jnp.einsum("tb,tnd->bnd", picker, per_tile, precision=lax.Precision.HIGHEST)
    return summed.reshape(-1, values.shape[-1])


def shards(
    nodes_in,
    edge_latents,
    src_block,
    src_offset,
    dst_block,
    dst_offset,
    tile_counts,
    w_edge1,
    b_edge1,
    w_edge2,
    b_edge2,
    w_node1,
    b_node1,
    w_node2,
    b_node2,
    cotangent,
):
    peers = lax.axis_size("nodes")
    myself = lax.axis_index("nodes")
    nodes = nodes_in[0]
    cot = cotangent[0]
    node_rows, width = nodes.shape
    tile = src_offset.shape[-1]
    slots = src_offset.shape[3]
    block_count = node_rows // tile
    tiles_all = peers * slots
    scale_factor = float(lax.axis_size("events") * peers * node_rows) ** (-0.5)
    w_src, w_dst, w_lat = (w_edge1[:width], w_edge1[width : 2 * width], w_edge1[2 * width :])
    w_own, w_agg = (w_node1[:width], w_node1[width:])
    send_blocks = src_block[0, 0].reshape(-1)
    send_hot = tile_onehot(src_offset[0, 0].reshape(tiles_all, tile), tile)
    recv_blocks = dst_block[0, 0].reshape(-1)
    recv_hot = tile_onehot(dst_offset[0, 0].reshape(tiles_all, tile), tile)
    outgoing = gather_tiles(nodes, send_blocks, send_hot).reshape(peers, slots, tile, width)
    h_src = lax.all_to_all(outgoing, "nodes", split_axis=0, concat_axis=0, tiled=True).reshape(
        -1, width
    )
    counts = lax.dynamic_index_in_dim(tile_counts[0], myself, 1, keepdims=False)
    live = jnp.arange(slots, dtype=jnp.int32)[None, :] < counts[:, None]
    live = (
        jnp.broadcast_to(live[..., None], (peers, slots, tile)).reshape(-1, 1).astype(jnp.bfloat16)
    )
    lat = edge_latents[0, 0].reshape(-1, width)
    h_dst = gather_tiles(nodes, recv_blocks, recv_hot).reshape(-1, width)
    z_one = (
        jnp.dot(h_src, w_src, preferred_element_type=jnp.float32)
        + jnp.dot(h_dst, w_dst, preferred_element_type=jnp.float32)
        + jnp.dot(lat, w_lat, preferred_element_type=jnp.float32)
        + b_edge1
    )
    a_one = jax.nn.silu(z_one).astype(jnp.bfloat16)
    message = (jnp.dot(a_one, w_edge2, preferred_element_type=jnp.float32) + b_edge2).astype(
        jnp.bfloat16
    ) * live
    agg = scatter_tiles(
        message.reshape(tiles_all, tile, width), recv_blocks, recv_hot, block_count
    ).astype(jnp.bfloat16)
    z_two = (
        jnp.dot(nodes, w_own, preferred_element_type=jnp.float32)
        + jnp.dot(agg, w_agg, preferred_element_type=jnp.float32)
        + b_node1
    )
    a_two = jax.nn.silu(z_two).astype(jnp.bfloat16)
    updated = (
        nodes.astype(jnp.float32)
        + jnp.dot(a_two, w_node2, preferred_element_type=jnp.float32)
        + b_node2
    ).astype(jnp.bfloat16)
    g_two = (
        jnp.dot(cot, w_node2.T, preferred_element_type=jnp.float32) * silu_slope(z_two)
    ).astype(jnp.bfloat16)
    node_terms = (
        jnp.concatenate(
            [
                jnp.dot(nodes.T, g_two, preferred_element_type=jnp.float32),
                jnp.dot(agg.T, g_two, preferred_element_type=jnp.float32),
            ],
            axis=0,
        ),
        jnp.sum(g_two.astype(jnp.float32), axis=0),
        jnp.dot(a_two.T, cot, preferred_element_type=jnp.float32),
        jnp.sum(cot.astype(jnp.float32), axis=0),
    )
    g_agg = jnp.dot(g_two, w_agg.T, preferred_element_type=jnp.float32).astype(jnp.bfloat16)
    g_msg = gather_tiles(g_agg, recv_blocks, recv_hot).reshape(-1, width) * live
    g_one = (
        jnp.dot(g_msg, w_edge2.T, preferred_element_type=jnp.float32) * silu_slope(z_one)
    ).astype(jnp.bfloat16)
    g_src = jnp.dot(g_one, w_src.T, preferred_element_type=jnp.float32).reshape(
        peers, slots, tile, width
    )
    returned = (
        lax.all_to_all(g_src.astype(jnp.bfloat16), "nodes", split_axis=0, concat_axis=0, tiled=True)
        .astype(g_src.dtype)
        .reshape(-1, width)
    )
    g_dst = jnp.dot(g_one, w_dst.T, preferred_element_type=jnp.float32)
    total = cot.astype(jnp.float32) + jnp.dot(g_two, w_own.T, preferred_element_type=jnp.float32)
    total = total + scatter_tiles(
        g_dst.reshape(tiles_all, tile, width), recv_blocks, recv_hot, block_count
    )
    total = total + scatter_tiles(
        returned.reshape(tiles_all, tile, width), send_blocks, send_hot, block_count
    )
    edge_terms = (
        jnp.concatenate(
            [
                jnp.dot(h_src.T, g_one, preferred_element_type=jnp.float32),
                jnp.dot(h_dst.T, g_one, preferred_element_type=jnp.float32),
                jnp.dot(lat.T, g_one, preferred_element_type=jnp.float32),
            ],
            axis=0,
        ),
        jnp.sum(g_one.astype(jnp.float32), axis=0),
        jnp.dot(a_one.T, g_msg, preferred_element_type=jnp.float32),
        jnp.sum(g_msg.astype(jnp.float32), axis=0),
    )
    summed = lax.psum(
        (
            edge_terms[0],
            edge_terms[1],
            edge_terms[2],
            edge_terms[3],
            node_terms[0],
            node_terms[1],
            node_terms[2],
            node_terms[3],
        ),
        ("events", "nodes"),
    )
    scaled = [value * scale_factor for value in summed]
    return (
        updated[None],
        total.astype(jnp.bfloat16)[None],
        scaled[0],
        scaled[1],
        scaled[2],
        scaled[3],
        scaled[4],
        scaled[5],
        scaled[6],
        scaled[7],
    )


def solution(mesh):
    return jax.shard_map(
        shards,
        mesh=mesh,
        in_specs=(
            P("events", "nodes", None),
            P("events", "nodes", None, None, None, None),
            P("events", "nodes", None, None),
            P("events", "nodes", None, None, None),
            P("events", "nodes", None, None),
            P("events", "nodes", None, None, None),
            P("events", None, None),
            P(),
            P(),
            P(),
            P(),
            P(),
            P(),
            P(),
            P(),
            P("events", "nodes", None),
        ),
        out_specs=(
            P("events", "nodes", None),
            P("events", "nodes", None),
            P(),
            P(),
            P(),
            P(),
            P(),
            P(),
            P(),
            P(),
        ),
        check_vma=False,
    )
```

profile of v0, /device:TPU:1, one launch (start us, length us, event | category | flops | bytes accessed | tf_op | source)
XLA Modules:
  0.0 243.8 jit_solution(3081769146235548526)
XLA Ops:
  8.1 1.7 gather_fusion
  9.8 1.3 convolution_convert_fusion.4
  11.1 5.4 %all-to-all-start = ((bf16[8,2,128,128]{3,2,1,0:T(8,128)(2,1)}), bf16[8,2,128,128]{3,2,1,0:T(8,128)(2,1)S(1)}, u32[]{:S(2)}, u32[]{:S(2)}) async-start(bf16[8,2,128,128]{3,2,1,0:T(8,128)(2,1)} %bitcast.6), calls=%async_computation | async-start | bytes 1048576 | tf_op jit(solution)/shard_map/all_to_all | solution.py:75
  20.9 1.2 fusion.25
  24.4 1.4 multiply_convert_fusion.1
  28.0 1.2 convolution_convert_fusion.5
  30.0 1.3 multiply_convert_fusion
  31.3 1.0 convert_reduce_fusion.1
  33.0 1.1 convolution_convert_fusion.1
  34.1 2.5 %gather_fusion.2 = bf16[16,128,128]{2,1,0:T(8,128)(2,1)} fusion(bf16[16,128,128]{2,1,0:T(8,128)(2,1)} %bitcast.107, s32[1024]{0:T(1024)S(1)} %pad_clamp_fusion), kind=kCustom, calls=%fused_computation.2 | custom fusion | bytes 1048640 | tf_op jit(solution)/shard_map/gather | solution.py:20
  36.5 2.3 convert_reduce_fusion.2
  40.8 1.0 convert_reduce_fusion.3
  43.4 1.1 convolution_convert_fusion
  46.5 1.1 fusion.11
  47.6 7.0 %all-to-all-start.1 = ((bf16[8,2,128,128]{3,2,1,0:T(8,128)(2,1)}), bf16[8,2,128,128]{3,2,1,0:T(8,128)(2,1)}, u32[]{:S(2)}, u32[]{:S(2)}) async-start(bf16[8,2,128,128]{3,2,1,0:T(8,128)(2,1)} %bitcast.104), calls=%async_computation.1 | async-start | bytes 1048576 | tf_op jit(solution)/shard_map/all_to_all | solution.py:133
  54.6 1.5 fusion.19
  56.2 2.2 fusion.15
  60.4 39.4 %all-reduce = (f32[128]{0:T(128)S(1)}, f32[128]{0:T(128)S(1)}, f32[128]{0:T(128)S(1)}, f32[128]{0:T(128)S(1)}) all-reduce(f32[128]{0:T(128)S(1)} %copy-done.26, f32[128]{0:T(128)S(1)} %copy-done.25, f32[128]{0:T(128)S(1)} %copy-done.24, f32[128]{0:T(128)S(1)} %copy-done.21), channel_id=1, replica_groups=mesh['events'=4,'nodes'=8] {'events','nodes'}, use_global_device_ids=true, to_apply=%region_2.3 | all-reduce | flops 512 | bytes 4096 | tf_op jit(solution)/shard_map/psum | solution.py:158
  100.4 1.6 copy.36
  102.5 126.7 %all-reduce.4.cloned.1.call-done = (f32[384,128]{1,0:T(8,128)}, f32[128,128]{1,0:T(8,128)}, f32[256,128]{1,0:T(8,128)}, f32[128,128]{1,0:T(8,128)}) async-done(((f32[384,128]{1,0:T(8,128)}, f32[128,128]{1,0:T(8,128)}, f32[256,128]{1,0:T(8,128)}, f32[128,128]{1,0:T(8,128)}), (f32[384,128]{1,0:T(8,128)}, f32[128,128]{1,0:T(8,128)}, f32[256,128]{1,0:T(8,128)}, ...) | async-done | bytes 458768 | tf_op jit(solution)/shard_map/psum | solution.py:158
  229.2 1.6 broadcast_multiply_fusion.1
  232.5 1.8 fusion.18
  234.2 1.2 fusion.13
  235.8 1.1 fusion.10
  (106 shorter events, 21.8 us)
Async XLA Ops:
  7.2 16.6 %copy-start = (bf16[1,1,8,2,128,128]{5,4,3,2,1,0:T(8,128)(2,1)S(1)}, bf16[1,1,8,2,128,128]{5,4,3,2,1,0:T(8,128)(2,1)}, u32[]{:S(2)}) copy-start(bf16[1,1,8,2,128,128]{5,4,3,2,1,0:T(8,128)(2,1)} %param.17) | copy-start | bytes 1572868
  8.1 1.7 copy-start.14
  11.1 6.2 %copy-start.1 = (bf16[1,2048,128]{2,1,0:T(8,128)(2,1)S(1)}, bf16[1,2048,128]{2,1,0:T(8,128)(2,1)}, u32[]{:S(2)}) copy-start(bf16[1,2048,128]{2,1,0:T(8,128)(2,1)} %param.16) | copy-start | bytes 1572868
  11.1 12.1 %all-to-all-start = ((bf16[8,2,128,128]{3,2,1,0:T(8,128)(2,1)}), bf16[8,2,128,128]{3,2,1,0:T(8,128)(2,1)S(1)}, u32[]{:S(2)}, u32[]{:S(2)}) async-start(bf16[8,2,128,128]{3,2,1,0:T(8,128)(2,1)} %bitcast.6), calls=%async_computation | async-start | bytes 1048576 | tf_op jit(solution)/shard_map/all_to_all | solution.py:75
  18.7 1.4 copy-start.2
  20.0 8.0 %copy-start.17 = (s32[16]{0:T(128)}, s32[16]{0:T(128)S(1)}, u32[]{:S(2)}) copy-start(s32[16]{0:T(128)S(1)} %eq.32) | copy-start | bytes 196
  20.9 2.2 copy-start.8
  24.4 1.5 copy-start.27
  25.8 1.1 copy-start.5
  28.0 1.4 copy-start.4
  30.0 1.3 copy-start.15
  38.8 1.0 copy-start.6
  38.8 2.0 copy-start.31
  42.5 0.9 copy-start.9
  44.5 1.0 copy-start.3
  45.5 1.0 copy-start.16
  45.5 1.0 copy-start.23
  47.6 184.8 %all-to-all-start.1 = ((bf16[8,2,128,128]{3,2,1,0:T(8,128)(2,1)}), bf16[8,2,128,128]{3,2,1,0:T(8,128)(2,1)}, u32[]{:S(2)}, u32[]{:S(2)}) async-start(bf16[8,2,128,128]{3,2,1,0:T(8,128)(2,1)} %bitcast.104), calls=%async_computation.1 | async-start | bytes 1048576 | tf_op jit(solution)/shard_map/all_to_all | solution.py:133
  54.6 174.6 %all-reduce.4.cloned.1.call-start = ((), (), s32[]{:S(2)}) async-start(), calls=%async_computation.2 | async-start | bytes 917504 | tf_op jit(solution)/shard_map/psum | solution.py:158
  54.6 1.5 copy-start.18
  229.2 1.6 copy-start.12
  229.2 1.6 copy-start.13
  230.8 1.0 copy-start.7
  232.4 1.8 copy-start.20
  (11 other events, 7.7 us)
Sparse Core Ops, SparseCore 0:
  100.0 129.1 all-reduce.3
where the time goes:
time: 245 us; the launch traced here: 244 us
  waiting for transfers between devices  128 us (52%)
  blocking collectives  39.4 us (16%)
  matrix products  28.1 us (11%)
  local copies, waits for them, and re-layouts  15.2 us (6%)
  between operations  14.3 us (6%)
  starting transfers between devices  12.4 us (5%)
  other arithmetic  6.65 us (3%)
    psum x1, waiting for transfers between devices, shards(): lax.psum((edge_terms[0], edge_terms[1], edge_terms[2], edge_terms[3], nod...  127 us
    psum x1, blocking collectives, shards(): lax.psum((edge_terms[0], edge_terms[1], edge_terms[2], edge_terms[3], nod...  39.4 us
    unnamed x66, local copies, waits for them, and re-layouts  7.1 us
    all_to_all x1, starting transfers between devices, shards(): lax.all_to_all(g_src.astype(jnp.bfloat16), 'nodes', split_axis=0, concat_...  7.01 us
    all_to_all x1, starting transfers between devices, shards(): lax.all_to_all(outgoing, 'nodes', split_axis=0, concat_axis=0, tiled=True)  5.35 us
  transfers between devices with their start and end apart: 3, of which 2 were waited for; matrix products, arithmetic and copies ran while one was open for 6% of the time, Pallas kernels for 0%

commit v1 on v0

--- a/solution.py
+++ b/solution.py
@@ -156,17 +156,20 @@
         jnp.sum(g_msg.astype(jnp.float32), axis=0),
     )
     summed = lax.psum(
-        (
-            edge_terms[0],
-            edge_terms[1],
-            edge_terms[2],
-            edge_terms[3],
-            node_terms[0],
-            node_terms[1],
-            node_terms[2],
-            node_terms[3],
-        ),
-        ("events", "nodes"),
+        lax.psum(
+            (
+                edge_terms[0],
+                edge_terms[1],
+                edge_terms[2],
+                edge_terms[3],
+                node_terms[0],
+                node_terms[1],
+                node_terms[2],
+                node_terms[3],
+            ),
+            "nodes",
+        ),
+        "events",
     )
     scaled = [value * scale_factor for value in summed]
     return (

time: 245 us -> 189 us (0.77)
  waiting for transfers between devices: 128 us -> 87.1 us
  blocking collectives: 39.4 us -> 22 us
    psum x1, waiting for transfers between devices: 127 us -> 50.3 us  [shards(): lax.psum((edge_terms[0], edge_terms[1], edge_terms[2], edge_terms[3], nod...]
    psum x0 -> x1, waiting for transfers between devices: none -> 35.6 us  [shards(): lax.psum(lax.psum((edge_terms[0], edge_terms[1], edge_terms[2], edge_term...]
    psum x1, blocking collectives: 39.4 us -> 11.6 us  [shards(): lax.psum((edge_terms[0], edge_terms[1], edge_terms[2], edge_terms[3], nod...]
    psum x0 -> x1, blocking collectives: none -> 10.4 us  [shards(): lax.psum(lax.psum((edge_terms[0], edge_terms[1], edge_terms[2], edge_term...]
    unnamed x66 -> x70, local copies, waits for them, and re-layouts: 7.1 us -> 8.4 us
  transfers between devices with their start and end apart: 3 -> 4, of which waited for: 2 -> 3; matrix products, arithmetic and copies ran while one was open for 6% -> 9% of each run, Pallas kernels for 0% -> 0%
where the time goes in v1:
time: 189 us; the launch traced here: 187 us
  waiting for transfers between devices  87.1 us (46%)
  matrix products  28.1 us (15%)
  blocking collectives  22 us (12%)
  local copies, waits for them, and re-layouts  16.4 us (9%)
  between operations  14.4 us (8%)
  starting transfers between devices  12.4 us (7%)
  other arithmetic  6.59 us (3%)
    psum x1, waiting for transfers between devices, shards(): lax.psum((edge_terms[0], edge_terms[1], edge_terms[2], edge_terms[3], nod...  50.3 us
    psum x1, waiting for transfers between devices, shards(): lax.psum(lax.psum((edge_terms[0], edge_terms[1], edge_terms[2], edge_term...  35.6 us
    psum x1, blocking collectives, shards(): lax.psum((edge_terms[0], edge_terms[1], edge_terms[2], edge_terms[3], nod...  11.6 us
    psum x1, blocking collectives, shards(): lax.psum(lax.psum((edge_terms[0], edge_terms[1], edge_terms[2], edge_term...  10.4 us
    unnamed x70, local copies, waits for them, and re-layouts  8.4 us
    all_to_all x1, starting transfers between devices, shards(): lax.all_to_all(g_src.astype(jnp.bfloat16), 'nodes', split_axis=0, concat_...  7.04 us
    all_to_all x1, starting transfers between devices, shards(): lax.all_to_all(outgoing, 'nodes', split_axis=0, concat_axis=0, tiled=True)  5.35 us
    gather x3, local copies, waits for them, and re-layouts, gather_tiles(): picked = table.reshape(-1, tile, table.shape[-1])[blocks]  4.81 us
  transfers between devices with their start and end apart: 4, of which 3 were waited for; matrix products, arithmetic and copies ran while one was open for 9% of the time, Pallas kernels for 0%

profile of v1, /device:TPU:1, one launch (start us, length us, event | category | flops | bytes accessed | tf_op | source)
XLA Modules:
  0.0 187.0 jit_solution(9945788451820599952)
XLA Ops:
  8.1 1.7 gather_fusion
  9.8 1.3 convolution_convert_fusion.4
  11.1 5.4 %all-to-all-start = ((bf16[8,2,128,128]{3,2,1,0:T(8,128)(2,1)}), bf16[8,2,128,128]{3,2,1,0:T(8,128)(2,1)S(1)}, u32[]{:S(2)}, u32[]{:S(2)}) async-start(bf16[8,2,128,128]{3,2,1,0:T(8,128)(2,1)} %bitcast.6), calls=%async_computation | async-start | bytes 1048576 | tf_op jit(solution)/shard_map/all_to_all | solution.py:75
  20.8 1.2 fusion.25
  22.0 1.1 all-to-all-done
  24.4 1.4 multiply_convert_fusion.1
  28.0 1.2 convolution_convert_fusion.5
  30.0 1.3 multiply_convert_fusion
  33.0 1.1 convolution_convert_fusion.1
  34.1 2.5 %gather_fusion.2 = bf16[16,128,128]{2,1,0:T(8,128)(2,1)} fusion(bf16[16,128,128]{2,1,0:T(8,128)(2,1)} %bitcast.107, s32[1024]{0:T(1024)S(1)} %pad_clamp_fusion), kind=kCustom, calls=%fused_computation.2 | custom fusion | bytes 1048640 | tf_op jit(solution)/shard_map/gather | solution.py:20
  36.5 2.3 %convert_reduce_fusion.2 = (f32[128]{0:T(128)}, bf16[16,128,128]{2,1,0:T(8,128)(2,1)S(1)}) fusion(bf16[16]{0:T(256)(128)(2,1)S(1)} %reshape.170, bf16[16,128,128]{2,1,0:T(8,128)(2,1)} %gather_fusion.2, s32[16,128]{1,0:T(8,128)S(1)} %bitcast.111), kind=kOutput, calls=%fused_computation.39 | convolution fusion | flops 68419456 | bytes 1057312 | tf_op jit(solution)/shard_map/ten,tnd->ted/dot_general | solution.py:21
  43.4 1.1 convolution_convert_fusion
  46.5 7.0 %all-to-all-start.1 = ((bf16[8,2,128,128]{3,2,1,0:T(8,128)(2,1)}), bf16[8,2,128,128]{3,2,1,0:T(8,128)(2,1)}, u32[]{:S(2)}, u32[]{:S(2)}) async-start(bf16[8,2,128,128]{3,2,1,0:T(8,128)(2,1)} %bitcast.104), calls=%async_computation.1 | async-start | bytes 1048576 | tf_op jit(solution)/shard_map/all_to_all | solution.py:133
  53.6 1.5 fusion.19
  55.1 2.2 %fusion.15 = f32[16,128,128]{2,0,1:T(8,128)} fusion(f32[16,128,128]{2,1,0:T(8,128)S(1)} %fusion.19, s32[16]{0:T(128)S(1)} %copy-done.19), kind=kOutput, calls=%fused_computation.35 | convolution fusion | flops 50331904 | bytes 2097216 | tf_op jit(solution)/shard_map/tb,tnd->bnd/dot_general | solution.py:36
  58.0 11.6 %all-reduce = (f32[128]{0:T(128)S(1)}, f32[128]{0:T(128)S(1)}, f32[128]{0:T(128)S(1)}, f32[128]{0:T(128)S(1)}) all-reduce(f32[128]{0:T(128)S(1)} %copy-done.28, f32[128]{0:T(128)S(1)} %copy-done.26, f32[128]{0:T(128)S(1)} %copy-done.25, f32[128]{0:T(128)S(1)} %copy-done.22), channel_id=1, replica_groups=mesh['events'=4,'nodes'=8] {'nodes'}, use_global_device_ids=true, to_apply=%region_3.4 | all-reduce | flops 512 | bytes 4096 | tf_op jit(solution)/shard_map/psum | solution.py:159
  69.6 10.4 %all-reduce.2 = (f32[128]{0:T(128)S(1)}, f32[128]{0:T(128)S(1)}, f32[128]{0:T(128)S(1)}, f32[128]{0:T(128)}) all-reduce(f32[128]{0:T(128)S(1)} %get-tuple-element.10, f32[128]{0:T(128)S(1)} %get-tuple-element.11, f32[128]{0:T(128)S(1)} %get-tuple-element.12, ...), channel_id=1, replica_groups=mesh['events'=4,'nodes'=8] {'events'}, use_global_device_ids=true, to_apply=%region_4.5 | all-reduce | flops 512 | bytes 4096 | tf_op jit(solution)/shard_map/psum | solution.py:158
  83.7 1.6 copy.36
  86.5 50.3 %all-reduce.7.cloned.1.call-done = (f32[384,128]{1,0:T(8,128)}, f32[128,128]{1,0:T(8,128)}, f32[256,128]{1,0:T(8,128)}, f32[128,128]{1,0:T(8,128)}) async-done(((f32[384,128]{1,0:T(8,128)}, f32[128,128]{1,0:T(8,128)}, f32[256,128]{1,0:T(8,128)}, f32[128,128]{1,0:T(8,128)}), (f32[384,128]{1,0:T(8,128)}, f32[128,128]{1,0:T(8,128)}, f32[256,128]{1,0:T(8,128)}, ...) | async-done | bytes 458768 | tf_op jit(solution)/shard_map/psum | solution.py:159
  136.8 1.8 fusion.18
  138.6 1.2 fusion.13
  140.2 1.1 fusion.10
  141.3 35.6 %all-reduce.9.cloned.1.call-done = (f32[384,128]{1,0:T(8,128)}, f32[128,128]{1,0:T(8,128)}, f32[256,128]{1,0:T(8,128)}, f32[128,128]{1,0:T(8,128)}) async-done(((f32[384,128]{1,0:T(8,128)}, f32[128,128]{1,0:T(8,128)}, f32[256,128]{1,0:T(8,128)}, f32[128,128]{1,0:T(8,128)}), (f32[384,128]{1,0:T(8,128)}, f32[128,128]{1,0:T(8,128)}, f32[256,128]{1,0:T(8,128)}, ...) | async-done | bytes 458768 | tf_op jit(solution)/shard_map/psum | solution.py:158
  176.9 1.7 broadcast_multiply_fusion
  (114 shorter events, 25.1 us)
Async XLA Ops:
  7.2 16.6 %copy-start = (bf16[1,1,8,2,128,128]{5,4,3,2,1,0:T(8,128)(2,1)S(1)}, bf16[1,1,8,2,128,128]{5,4,3,2,1,0:T(8,128)(2,1)}, u32[]{:S(2)}) copy-start(bf16[1,1,8,2,128,128]{5,4,3,2,1,0:T(8,128)(2,1)} %param.17) | copy-start | bytes 1572868
  8.1 1.7 copy-start.15
  11.1 6.2 %copy-start.1 = (bf16[1,2048,128]{2,1,0:T(8,128)(2,1)S(1)}, bf16[1,2048,128]{2,1,0:T(8,128)(2,1)}, u32[]{:S(2)}) copy-start(bf16[1,2048,128]{2,1,0:T(8,128)(2,1)} %param.16) | copy-start | bytes 1572868
  11.1 12.1 %all-to-all-start = ((bf16[8,2,128,128]{3,2,1,0:T(8,128)(2,1)}), bf16[8,2,128,128]{3,2,1,0:T(8,128)(2,1)S(1)}, u32[]{:S(2)}, u32[]{:S(2)}) async-start(bf16[8,2,128,128]{3,2,1,0:T(8,128)(2,1)} %bitcast.6), calls=%async_computation | async-start | bytes 1048576 | tf_op jit(solution)/shard_map/all_to_all | solution.py:75
  18.7 1.3 copy-start.2
  19.8 8.1 %copy-start.18 = (s32[16]{0:T(128)}, s32[16]{0:T(128)S(1)}, u32[]{:S(2)}) copy-start(s32[16]{0:T(128)S(1)} %eq.32) | copy-start | bytes 196
  20.8 2.4 %copy-start.8 = (bf16[384,128]{1,0:T(8,128)(2,1)S(1)}, bf16[384,128]{1,0:T(8,128)(2,1)}, u32[]{:S(2)}) copy-start(bf16[384,128]{1,0:T(8,128)(2,1)} %param.23) | copy-start | bytes 294916
  24.4 1.5 copy-start.29
  25.8 1.1 copy-start.6
  28.0 1.4 copy-start.5
  30.0 1.3 copy-start.16
  38.8 1.0 copy-start.7
  38.8 2.0 %copy-start.33 = (f32[2048,128]{1,0:T(8,128)S(1)}, f32[2048,128]{1,0:T(8,128)}, u32[]{:S(2)}) copy-start(f32[2048,128]{1,0:T(8,128)} %get-tuple-element.27) | copy-start | bytes 3145732
  42.5 0.9 copy-start.9
  44.5 1.0 copy-start.3
  46.5 90.3 %all-to-all-start.1 = ((bf16[8,2,128,128]{3,2,1,0:T(8,128)(2,1)}), bf16[8,2,128,128]{3,2,1,0:T(8,128)(2,1)}, u32[]{:S(2)}, u32[]{:S(2)}) async-start(bf16[8,2,128,128]{3,2,1,0:T(8,128)(2,1)} %bitcast.104), calls=%async_computation.1 | async-start | bytes 1048576 | tf_op jit(solution)/shard_map/all_to_all | solution.py:133
  53.6 83.2 %all-reduce.7.cloned.1.call-start = ((), (), s32[]{:S(2)}) async-start(), calls=%async_computation.2 | async-start | bytes 917504 | tf_op jit(solution)/shard_map/psum | solution.py:159
  53.6 1.5 copy-start.19
  55.1 2.2 %copy-start.28 = (f32[128]{0:T(128)S(1)}, f32[128]{0:T(128)}, u32[]{:S(2)}) copy-start(f32[128]{0:T(128)} %get-tuple-element.30) | copy-start | bytes 1540
  80.5 1.4 copy-start.4
  81.9 95.0 %all-reduce.9.cloned.1.call-start = ((), (), s32[]{:S(2)}) async-start(), calls=%async_computation.3 | async-start | bytes 917504 | tf_op jit(solution)/shard_map/psum | solution.py:158
  136.8 1.8 copy-start.21
  176.9 1.7 copy-start.11
  178.6 0.9 copy-start.14
  (14 other events, 9.9 us)
Sparse Core Ops, SparseCore 0:
  82.0 54.7 all-reduce.6
  139.4 37.4 all-reduce.8
